TPU v7x, 32 devices: a whole 2x2x4 slice. The times are simulated.
32 devices in a mesh: groups: 2 (over y), front: 4 (over z), batch: 2 (over x), line: 2 (over core).
Axes of the slice: x: 2, y: 2, z: 4, core: 2. Of those that a mesh axis runs over, the one named last changes fastest.
Arguments:
- injections: float32 [2048, 512], P('front', ('groups', 'batch')), parts along dimension 1, may hold values from -6 to 6
- switch_from: int32 [2, 512], P(None, ('groups', 'batch')), parts along dimension 1, may hold values from 0 to 2047
- switch_to: int32 [2, 512], P(None, ('groups', 'batch')), parts along dimension 1, may hold values from 0 to 2047
- switch_susc: float32 [2, 512], P(None, ('groups', 'batch')), parts along dimension 1, may hold values from 0.5 to 4
- coupling: float32 [2048, 512], P('front'), may hold values from -1 to 1
- pivot_inverse: float32 [2048, 512], P('front')
- branch_from: int32 [4096], P(('front', 'line')), may hold values from 0 to 2047, as said below
- branch_to: int32 [4096], P(('front', 'line')), may hold values from 0 to 2047, as said below
- branch_susc: float32 [4096], P(('front', 'line')), may hold values from 0.5 to 2
- branch_owner: int32 [4096, 1], P(('front', 'line')), may hold values from 0 to 7; in each aligned block of 512 rows (0 to 511, 512 to 1023, ...) at most 128 rows name the same one
- in_weight: float32 [128], replicated, may hold values from -4 to 4
- in_bias: float32 [128], replicated, may hold values from -1 to 1
- out_weight: bfloat16 [128, 128], replicated, may hold values from -0.5 to 0.5
Outputs:
- region_scores: bfloat16 [8, 512, 128], P(('front', 'line'), ('groups', 'batch')), parts along dimension 1
- angles: float32 [2048, 512], P('front', ('groups', 'batch')), parts along dimension 1
There are 2 independent parts, one for each index of `groups`. A program takes and returns all parts, laid end to end along the dimension named above; an argument that names none is the same for every part. Nothing has to cross between parts.
Inputs may be any that keep to these rules, and one draw needn't show every extreme that they name: `branch_from`: the bus of row r lies in slab s = r // 1024, between s * 512 and s * 512 + 511. `branch_to`: the bus of row r lies in slab s = r // 1024 or in slab s + 1. `branch_owner`: in each aligned block of 512 rows (the branches of one device) no owner is named by more than 128 rows.
All inputs are finite; a program needn't handle non-finite values.
Results may differ from a plain program's by a relative error of at most 0.005.
Values sent between devices are 32-bit elements; how exact they have to be, the bound alone decides.
A program may use at most 64 MiB of HBM per device.

v0:
```python
import jax
import jax.numpy as jnp
from jax import lax
from jax.sharding import PartitionSpec as P

K = 2
BR_DEV = 512


def from_behind(value, axis, by):
    count = lax.axis_size(axis)
    pairs = [(i, i + by) for i in range(count) if 0 <= i + by < count]
    return lax.ppermute(value, axis, pairs)


def product(operand, against):
    return jnp.dot(
        operand, against, precision=lax.Precision.HIGHEST, preferred_element_type=jnp.float32
    )


def centered_tanh(loadings, in_weight, in_bias):
    return jnp.tanh(loadings[..., None] * in_weight + in_bias) - jnp.tanh(in_bias)


def capacitance_solve(terms, switch_susc):
    switches = switch_susc.shape[0]
    factor = [[None] * switches for row_at in range(switches)]
    for row_at in range(switches):
        for col_at in range(row_at + 1):
            partial_sum = terms[row_at, 1 + col_at]
            if row_at == col_at:
                partial_sum = partial_sum + 1.0 / switch_susc[row_at]
            for inner_at in range(col_at):
                partial_sum = partial_sum - factor[row_at][inner_at] * factor[col_at][inner_at]
            if row_at == col_at:
                factor[row_at][col_at] = jnp.sqrt(partial_sum)
            else:
                factor[row_at][col_at] = partial_sum / factor[col_at][col_at]
    lower_part = []
    for row_at in range(switches):
        running = terms[row_at, 0]
        for inner_at in range(row_at):
            running = running - factor[row_at][inner_at] * lower_part[inner_at]
        lower_part.append(running / factor[row_at][row_at])
    weights = [None] * switches
    for row_at in reversed(range(switches)):
        running = lower_part[row_at]
        for inner_at in range(row_at + 1, switches):
            running = running - factor[inner_at][row_at] * weights[inner_at]
        weights[row_at] = running / factor[row_at][row_at]
    return jnp.stack(weights)


def body(
    injections,
    switch_from,
    switch_to,
    switch_susc,
    coupling,
    pivot_inverse,
    branch_from,
    branch_to,
    branch_susc,
    branch_owner,
    in_weight,
    in_bias,
    out_weight,
):
    fronts = lax.axis_size("front")
    front_at = lax.axis_index("front")
    slab_size = coupling.shape[1]
    topo_count = injections.shape[1]
    first_bus = front_at * slab_size
    bus_ids = first_bus + jnp.arange(slab_size, dtype=jnp.int32)
    from_hot = (bus_ids[:, None, None] == switch_from[None]).astype(jnp.float32)
    to_hot = (bus_ids[:, None, None] == switch_to[None]).astype(jnp.float32)
    incidence = from_hot - to_hot
    stacked = jnp.concatenate([injections[:, None, :], incidence], axis=1).reshape(slab_size, -1)

    def lower_step(step_at, current):
        arrived = from_behind(current, "front", 1)
        return stacked - product(coupling, arrived)

    lowered = lax.fori_loop(0, fronts - 1, lower_step, stacked)
    pivoted = product(pivot_inverse, lowered)

    def upper_step(step_at, current):
        arrived = from_behind(product(coupling.T, current), "front", -1)
        return pivoted - arrived

    solved = lax.fori_loop(0, fronts - 1, upper_step, pivoted)
    solved_cols = solved.reshape(slab_size, K + 1, topo_count)
    local_terms = jnp.einsum(
        "bit,bct->ict", incidence, solved_cols, precision=lax.Precision.HIGHEST
    )
    terms = lax.psum(local_terms, "front")
    weights = capacitance_solve(terms, switch_susc)
    angles = solved_cols[:, 0, :] - jnp.einsum(
        "bit,it->bt", solved_cols[:, 1:, :], weights, precision=lax.Precision.HIGHEST
    )
    following = from_behind(angles, "front", -1)
    joined = jnp.concatenate([angles, following], axis=0)
    flows = branch_susc[:, None] * (joined[branch_from - first_bus] - joined[branch_to - first_bus])
    owners = lax.axis_size(("front", "line"))
    capacity = 2 * BR_DEV // owners
    owner_ids = branch_owner[:, 0]
    owner_hot = (owner_ids[:, None] == jnp.arange(owners, dtype=jnp.int32)[None]).astype(jnp.int32)
    before = jnp.cumsum(owner_hot, axis=0) - owner_hot
    position = jnp.sum(before * owner_hot, axis=1)
    slot_ids = owner_ids * capacity + position
    dispatch = (jnp.arange(owners * capacity, dtype=jnp.int32)[:, None] == slot_ids[None]).astype(
        jnp.float32
    )
    outgoing = product(dispatch, flows).reshape(owners, capacity, topo_count)
    arrived = lax.all_to_all(outgoing, ("front", "line"), split_axis=0, concat_axis=0, tiled=True)
    slot_rows = arrived.reshape(-1, arrived.shape[2])
    span_size = 32
    blocks = slot_rows.reshape(-1, span_size, slot_rows.shape[1])

    def accumulate(running, slot_block):
        return (running + jnp.sum(centered_tanh(slot_block, in_weight, in_bias), axis=0), None)

    start_sum = jnp.zeros((slot_rows.shape[1], in_weight.shape[0]), jnp.float32)
    summed, unused = lax.scan(accumulate, start_sum, blocks)
    pooled = (summed * BR_DEV ** (-0.5)).astype(jnp.bfloat16)
    region_scores = jnp.dot(pooled, out_weight, preferred_element_type=jnp.float32).astype(
        jnp.bfloat16
    )
    return (region_scores[None], angles)


def solution(mesh):
    in_specs = (
        P("front", ("groups", "batch")),
        P(None, ("groups", "batch")),
        P(None, ("groups", "batch")),
        P(None, ("groups", "batch")),
        P("front", None),
        P("front", None),
        P(("front", "line")),
        P(("front", "line")),
        P(("front", "line")),
        P(("front", "line"), None),
        P(),
        P(),
        P(),
    )
    out_specs = (P(("front", "line"), ("groups", "batch"), None), P("front", ("groups", "batch")))
    return jax.shard_map(body, mesh=mesh, in_specs=in_specs, out_specs=out_specs, check_vma=False)
```

profile of v0, /device:TPU:0, one launch (start us, length us, event | category | flops | bytes accessed | tf_op | source)
XLA Modules:
  0.0 243.3 jit_solution(18174583019754320143)
XLA Ops:
  4.5 73.9 %while.32 = (s32[]{:T(128)}, f32[512,384]{1,0:T(8,128)}, f32[512,512]{1,0:T(8,128)S(1)}, f32[512,384]{1,0:T(8,128)S(1)}, s32[]{:T(128)}) while((s32[]{:T(128)}, f32[512,384]{1,0:T(8,128)}, f32[512,512]{1,0:T(8,128)S(1)}, f32[512,384]{1,0:T(8,128)S(1)}, s32[]{:T(128)}) %tuple.77), condition=%wide.region_4.0_spmd, body=%wide.region_3.0_spmd.sunk | while | flops 1208156160 | bytes 6553701 | solution.py:85
  4.5 5.8 %collective-permute-start = (f32[512,384]{1,0:T(8,128)}, f32[512,384]{1,0:T(8,128)}, u32[]{:S(2)}, u32[]{:S(2)}) collective-permute-start(f32[512,384]{1,0:T(8,128)} %get-tuple-element.274), channel_id=1, source_target_pairs={{0,4},{4,8},{8,12},{1,5},{5,9},{9,13},{2,6},{6,10},{10,14},{3,7},{... | collective-permute-start | bytes 2359304 | tf_op jit(solution)/shard_map/while/body/eval_jaxpr/ppermute | solution.py:13
  10.3 16.2 %collective-permute-done = f32[512,384]{1,0:T(8,128)} collective-permute-done((f32[512,384]{1,0:T(8,128)}, f32[512,384]{1,0:T(8,128)}, u32[]{:S(2)}, u32[]{:S(2)}) %collective-permute-start) | collective-permute-done | bytes 786464 | tf_op jit(solution)/shard_map/while/body/eval_jaxpr/ppermute | solution.py:13
  26.6 3.8 %convolution_subtract_fusion.2 = f32[512,384]{1,0:T(8,128)} fusion(f32[512,384]{1,0:T(8,128)S(1)} %get-tuple-element.281, f32[512,512]{1,0:T(8,128)S(1)} %get-tuple-element.280, f32[512,384]{1,0:T(8,128)} %collective-permute-done), kind=kOutput, calls=%fused_computation.2.clone.1 | convolution fusion | flops 1208156160 | bytes 3407872 | tf_op jit(solution)/shard_map/while/body/eval_jaxpr/dot_general | solution.py:17
  30.4 5.3 %collective-permute-start = (f32[512,384]{1,0:T(8,128)}, f32[512,384]{1,0:T(8,128)}, u32[]{:S(2)}, u32[]{:S(2)}) collective-permute-start(f32[512,384]{1,0:T(8,128)} %get-tuple-element.274), channel_id=1, source_target_pairs={{0,4},{4,8},{8,12},{1,5},{5,9},{9,13},{2,6},{6,10},{10,14},{3,7},{... | collective-permute-start | bytes 2359304 | tf_op jit(solution)/shard_map/while/body/eval_jaxpr/ppermute | solution.py:13
  35.7 15.4 %collective-permute-done = f32[512,384]{1,0:T(8,128)} collective-permute-done((f32[512,384]{1,0:T(8,128)}, f32[512,384]{1,0:T(8,128)}, u32[]{:S(2)}, u32[]{:S(2)}) %collective-permute-start) | collective-permute-done | bytes 786464 | tf_op jit(solution)/shard_map/while/body/eval_jaxpr/ppermute | solution.py:13
  51.0 3.8 %convolution_subtract_fusion.2 = f32[512,384]{1,0:T(8,128)} fusion(f32[512,384]{1,0:T(8,128)S(1)} %get-tuple-element.281, f32[512,512]{1,0:T(8,128)S(1)} %get-tuple-element.280, f32[512,384]{1,0:T(8,128)} %collective-permute-done), kind=kOutput, calls=%fused_computation.2.clone.1 | convolution fusion | flops 1208156160 | bytes 3407872 | tf_op jit(solution)/shard_map/while/body/eval_jaxpr/dot_general | solution.py:17
  54.9 5.3 %collective-permute-start = (f32[512,384]{1,0:T(8,128)}, f32[512,384]{1,0:T(8,128)}, u32[]{:S(2)}, u32[]{:S(2)}) collective-permute-start(f32[512,384]{1,0:T(8,128)} %get-tuple-element.274), channel_id=1, source_target_pairs={{0,4},{4,8},{8,12},{1,5},{5,9},{9,13},{2,6},{6,10},{10,14},{3,7},{... | collective-permute-start | bytes 2359304 | tf_op jit(solution)/shard_map/while/body/eval_jaxpr/ppermute | solution.py:13
  60.1 14.4 %collective-permute-done = f32[512,384]{1,0:T(8,128)} collective-permute-done((f32[512,384]{1,0:T(8,128)}, f32[512,384]{1,0:T(8,128)}, u32[]{:S(2)}, u32[]{:S(2)}) %collective-permute-start) | collective-permute-done | bytes 786464 | tf_op jit(solution)/shard_map/while/body/eval_jaxpr/ppermute | solution.py:13
  74.5 3.8 %convolution_subtract_fusion.2 = f32[512,384]{1,0:T(8,128)} fusion(f32[512,384]{1,0:T(8,128)S(1)} %get-tuple-element.281, f32[512,512]{1,0:T(8,128)S(1)} %get-tuple-element.280, f32[512,384]{1,0:T(8,128)} %collective-permute-done), kind=kOutput, calls=%fused_computation.2.clone.1 | convolution fusion | flops 1208156160 | bytes 3407872 | tf_op jit(solution)/shard_map/while/body/eval_jaxpr/dot_general | solution.py:17
  78.4 4.7 %convolution_bitcast_fusion = f32[512,384]{0,1:T(8,128)} fusion(f32[512,384]{1,0:T(8,128)} %get-tuple-element.98, f32[512,512]{1,0:T(8,128)S(1)} %copy-done), kind=kOutput, calls=%fused_computation.8 | convolution fusion | flops 1207959552 | bytes 2621440 | tf_op jit(solution)/shard_map/dot_general | solution.py:17
  85.4 72.7 %while.33 = (s32[]{:T(128)}, f32[512,384]{1,0:T(8,128)}, f32[512,512]{1,0:T(8,128)S(1)}, f32[512,384]{1,0:T(8,128)S(1)}, s32[]{:T(128)}) while((s32[]{:T(128)}, f32[512,384]{1,0:T(8,128)}, f32[512,512]{1,0:T(8,128)S(1)}, f32[512,384]{1,0:T(8,128)S(1)}, s32[]{:T(128)}) %tuple.78), condition=%wide.region_6.7_spmd, body=%wide.region_5.0_spmd.sunk | while | flops 1208156160 | bytes 8126565 | solution.py:92
  85.4 3.8 %fusion.37 = f32[512,384]{1,0:T(8,128)} fusion(f32[512,512]{1,0:T(8,128)S(1)} %get-tuple-element.295, f32[512,384]{1,0:T(8,128)} %get-tuple-element.289), kind=kOutput, calls=%fused_computation.57.clone.1 | convolution fusion | flops 1207959552 | bytes 2621440 | tf_op jit(solution)/shard_map/while/body/eval_jaxpr/dot_general | solution.py:17
  90.5 18.2 %collective-permute-done.1 = f32[512,384]{1,0:T(8,128)} collective-permute-done((f32[512,384]{1,0:T(8,128)}, f32[512,384]{1,0:T(8,128)}, u32[]{:S(2)}, u32[]{:S(2)}) %collective-permute-start.1) | collective-permute-done | bytes 786464 | tf_op jit(solution)/shard_map/while/body/eval_jaxpr/ppermute | solution.py:13
  110.8 3.8 %fusion.37 = f32[512,384]{1,0:T(8,128)} fusion(f32[512,512]{1,0:T(8,128)S(1)} %get-tuple-element.295, f32[512,384]{1,0:T(8,128)} %get-tuple-element.289), kind=kOutput, calls=%fused_computation.57.clone.1 | convolution fusion | flops 1207959552 | bytes 2621440 | tf_op jit(solution)/shard_map/while/body/eval_jaxpr/dot_general | solution.py:17
  116.0 16.8 %collective-permute-done.1 = f32[512,384]{1,0:T(8,128)} collective-permute-done((f32[512,384]{1,0:T(8,128)}, f32[512,384]{1,0:T(8,128)}, u32[]{:S(2)}, u32[]{:S(2)}) %collective-permute-start.1) | collective-permute-done | bytes 786464 | tf_op jit(solution)/shard_map/while/body/eval_jaxpr/ppermute | solution.py:13
  134.9 3.8 %fusion.37 = f32[512,384]{1,0:T(8,128)} fusion(f32[512,512]{1,0:T(8,128)S(1)} %get-tuple-element.295, f32[512,384]{1,0:T(8,128)} %get-tuple-element.289), kind=kOutput, calls=%fused_computation.57.clone.1 | convolution fusion | flops 1207959552 | bytes 2621440 | tf_op jit(solution)/shard_map/while/body/eval_jaxpr/dot_general | solution.py:17
  140.0 15.9 %collective-permute-done.1 = f32[512,384]{1,0:T(8,128)} collective-permute-done((f32[512,384]{1,0:T(8,128)}, f32[512,384]{1,0:T(8,128)}, u32[]{:S(2)}, u32[]{:S(2)}) %collective-permute-start.1) | collective-permute-done | bytes 786464 | tf_op jit(solution)/shard_map/while/body/eval_jaxpr/ppermute | solution.py:13
  159.4 4.5 %convolution_bitcast_fusion.1 = f32[2,3,128]{1,0,2:T(2,128)S(1)} fusion(f32[512,3,128]{0,2,1:T(8,128)S(1)} %bitcast.81, f32[512,2,128]{0,2,1:T(8,128)S(1)} %convert_subtract_fusion), kind=kOutput, calls=%fused_computation.9 | convolution fusion | flops 4718592 | bytes 1313792 | tf_op jit(solution)/shard_map/bit,bct->ict/dot_general | solution.py:94
  163.9 19.6 %psum.7 = f32[2,3,128]{1,0,2:T(2,128)S(1)} all-reduce(f32[2,3,128]{1,0,2:T(2,128)S(1)} %convolution_bitcast_fusion.1), channel_id=1, replica_groups=mesh['groups'=2,'front'=4,'batch'=2,'line'=2] {'front'}, use_global_device_ids=true, to_apply=%region_7.8 | all-reduce | flops 768 | bytes 6144 | tf_op jit(solution)/shard_map/psum | solution.py:97
  189.1 5.4 %collective-permute-done.2 = f32[512,128]{1,0:T(8,128)S(1)} collective-permute-done((f32[512,128]{1,0:T(8,128)S(1)}, f32[512,128]{1,0:T(8,128)S(1)}, u32[]{:S(2)}, u32[]{:S(2)}) %collective-permute-start.2) | collective-permute-done | bytes 262176 | tf_op jit(solution)/shard_map/ppermute | solution.py:13
  198.6 3.5 %all-to-all-start = ((f32[8,128,128]{2,1,0:T(8,128)}), f32[8,128,128]{2,1,0:T(8,128)S(1)}, u32[]{:S(2)}, u32[]{:S(2)}) async-start(f32[8,128,128]{2,1,0:T(8,128)} %bitcast.13), calls=%async_computation | async-start | bytes 1048576 | tf_op jit(solution)/shard_map/all_to_all | solution.py:116
  202.1 15.2 %all-to-all-done = f32[8,128,128]{2,1,0:T(8,128)S(1)} async-done(((f32[8,128,128]{2,1,0:T(8,128)}), f32[8,128,128]{2,1,0:T(8,128)S(1)}, u32[]{:S(2)}, u32[]{:S(2)}) %all-to-all-start) | async-done | bytes 524320 | tf_op jit(solution)/shard_map/all_to_all | solution.py:116
  217.4 25.2 %while.34 = (s32[]{:T(128)}, f32[128,128]{1,0:T(8,128)S(1)}, f32[32,32,128]{2,1,0:T(8,128)S(1)}, f32[128]{0:T(128)S(1)}, f32[128]{0:T(128)S(1)}, /*index=5*/f32[1,1,128]{2,1,0:T(1,128)S(1)}, s32[]{:T(128)}, s32[]{:T(128)}) while((s32[]{:T(128)}, f32[128,128]{1,0:T(8,128)S(1)}, f32[32,32,128]{2,1,0:T(8,128)S(1)}, ...), condition=%wide.region_10.11_spmd.clone, body=%wide.region_8.10_spmd.clone.sunk | while | flops 2113539 | bytes 312931 | solution.py:125
  (160 shorter events, 51.8 us)
Async XLA Ops:
  0.6 77.8 %copy-start = (f32[512,512]{1,0:T(8,128)S(1)}, f32[512,512]{1,0:T(8,128)}, u32[]{:S(2)}) copy-start(f32[512,512]{1,0:T(8,128)} %param.24) | copy-start | bytes 3145732
  3.0 1.5 copy-start.1
  4.5 22.0 %collective-permute-start = (f32[512,384]{1,0:T(8,128)}, f32[512,384]{1,0:T(8,128)}, u32[]{:S(2)}, u32[]{:S(2)}) collective-permute-start(f32[512,384]{1,0:T(8,128)} %get-tuple-element.274), channel_id=1, source_target_pairs={{0,4},{4,8},{8,12},{1,5},{5,9},{9,13},{2,6},{6,10},{10,14},{3,7},{... | collective-permute-start | bytes 2359304 | tf_op jit(solution)/shard_map/while/body/eval_jaxpr/ppermute | solution.py:13
  30.4 20.6 %collective-permute-start = (f32[512,384]{1,0:T(8,128)}, f32[512,384]{1,0:T(8,128)}, u32[]{:S(2)}, u32[]{:S(2)}) collective-permute-start(f32[512,384]{1,0:T(8,128)} %get-tuple-element.274), channel_id=1, source_target_pairs={{0,4},{4,8},{8,12},{1,5},{5,9},{9,13},{2,6},{6,10},{10,14},{3,7},{... | collective-permute-start | bytes 2359304 | tf_op jit(solution)/shard_map/while/body/eval_jaxpr/ppermute | solution.py:13
  54.9 19.7 %collective-permute-start = (f32[512,384]{1,0:T(8,128)}, f32[512,384]{1,0:T(8,128)}, u32[]{:S(2)}, u32[]{:S(2)}) collective-permute-start(f32[512,384]{1,0:T(8,128)} %get-tuple-element.274), channel_id=1, source_target_pairs={{0,4},{4,8},{8,12},{1,5},{5,9},{9,13},{2,6},{6,10},{10,14},{3,7},{... | collective-permute-start | bytes 2359304 | tf_op jit(solution)/shard_map/while/body/eval_jaxpr/ppermute | solution.py:13
  89.2 19.5 %collective-permute-start.1 = (f32[512,384]{1,0:T(8,128)}, f32[512,384]{1,0:T(8,128)}, u32[]{:S(2)}, u32[]{:S(2)}) collective-permute-start(f32[512,384]{1,0:T(8,128)} %fusion.37), channel_id=1, source_target_pairs={{4,0},{8,4},{12,8},{5,1},{9,5},{13,9},{6,2},{10,6},{14,10},{7,3},{... | collective-permute-start | bytes 2359304 | tf_op jit(solution)/shard_map/while/body/eval_jaxpr/ppermute | solution.py:13
  114.7 18.1 %collective-permute-start.1 = (f32[512,384]{1,0:T(8,128)}, f32[512,384]{1,0:T(8,128)}, u32[]{:S(2)}, u32[]{:S(2)}) collective-permute-start(f32[512,384]{1,0:T(8,128)} %fusion.37), channel_id=1, source_target_pairs={{4,0},{8,4},{12,8},{5,1},{9,5},{13,9},{6,2},{10,6},{14,10},{7,3},{... | collective-permute-start | bytes 2359304 | tf_op jit(solution)/shard_map/while/body/eval_jaxpr/ppermute | solution.py:13
  138.7 17.2 %collective-permute-start.1 = (f32[512,384]{1,0:T(8,128)}, f32[512,384]{1,0:T(8,128)}, u32[]{:S(2)}, u32[]{:S(2)}) collective-permute-start(f32[512,384]{1,0:T(8,128)} %fusion.37), channel_id=1, source_target_pairs={{4,0},{8,4},{12,8},{5,1},{9,5},{13,9},{6,2},{10,6},{14,10},{7,3},{... | collective-permute-start | bytes 2359304 | tf_op jit(solution)/shard_map/while/body/eval_jaxpr/ppermute | solution.py:13
  163.9 21.8 %copy-start.8 = (f32[2,128]{1,0:T(2,128)S(1)}, f32[2,128]{1,0:T(2,128)}, u32[]{:S(2)}) copy-start(f32[2,128]{1,0:T(2,128)} %param.22) | copy-start | bytes 3076
  185.9 1.7 copy-start.6
  185.9 1.7 copy-start.7
  185.9 1.7 copy-start.4
  186.2 9.4 %copy-start.2 = (f32[512,128]{1,0:T(8,128)}, f32[512,128]{1,0:T(8,128)S(1)}, u32[]{:S(2)}) copy-start(f32[512,128]{1,0:T(8,128)S(1)} %bitcast_subtract_fusion) | copy-start | bytes 786436
  186.2 8.3 %collective-permute-start.2 = (f32[512,128]{1,0:T(8,128)S(1)}, f32[512,128]{1,0:T(8,128)S(1)}, u32[]{:S(2)}, u32[]{:S(2)}) collective-permute-start(f32[512,128]{1,0:T(8,128)S(1)} %bitcast_subtract_fusion), channel_id=1, source_target_pairs={{4,0},{8,4},{12,8},{5,1},{9,5},{13,9},{6,2},{10,6},{14,10},{7,3},{... | collective-permute-start | bytes 786440 | tf_op jit(solution)/shard_map/ppermute | solution.py:13
  195.6 1.1 copy-start.5
  196.7 5.5 %copy-start.10 = (f32[128]{0:T(128)S(1)}, f32[128]{0:T(128)}, u32[]{:S(2)}) copy-start(f32[128]{0:T(128)} %param.30) | copy-start | bytes 1540
  196.7 20.7 %copy-start.9 = (f32[128]{0:T(128)S(1)}, f32[128]{0:T(128)}, u32[]{:S(2)}) copy-start(f32[128]{0:T(128)} %param.29) | copy-start | bytes 1540
  198.6 18.8 %all-to-all-start = ((f32[8,128,128]{2,1,0:T(8,128)}), f32[8,128,128]{2,1,0:T(8,128)S(1)}, u32[]{:S(2)}, u32[]{:S(2)}) async-start(f32[8,128,128]{2,1,0:T(8,128)} %bitcast.13), calls=%async_computation | async-start | bytes 1048576 | tf_op jit(solution)/shard_map/all_to_all | solution.py:116
  217.4 25.2 %copy-start.3 = (bf16[128,128]{1,0:T(8,128)(2,1)S(1)}, bf16[128,128]{1,0:T(8,128)(2,1)}, u32[]{:S(2)}) copy-start(bf16[128,128]{1,0:T(8,128)(2,1)} %param.31) | copy-start | bytes 98308
where the time goes:
time: 244 us; the launch traced here: 243 us
  waiting for transfers between devices  118 us (48%)
  matrix products  34.9 us (14%)
  other arithmetic  32.3 us (13%)
  starting transfers between devices  24.9 us (10%)
  blocking collectives  19.6 us (8%)
  local copies, waits for them, and re-layouts  11.7 us (5%)
    ppermute x7, waiting for transfers between devices, from_behind(): return lax.ppermute(value, axis, pairs)  102 us
    dot_general x8, matrix products, product(): jnp.dot(operand, against, precision=lax.Precision.HIGHEST, preferred_elem...  29.7 us
    reduce_sum x32, other arithmetic, accumulate(): jnp.sum(centered_tanh(slot_block, in_weight, in_bias), axis=0)  23 us
    ppermute x7, starting transfers between devices, from_behind(): return lax.ppermute(value, axis, pairs)  21.5 us
    psum x1, blocking collectives, body(): terms = lax.psum(local_terms, 'front')  19.6 us
    all_to_all x1, waiting for transfers between devices, body(): lax.all_to_all(outgoing, ('front', 'line'), split_axis=0, concat_axis=0,...  15.2 us
    sub x3, other arithmetic, upper_step(): return pivoted - arrived  6.31 us
  transfers between devices with their start and end apart: 8, of which 8 were waited for; matrix products, arithmetic and copies ran while one was open for 1% of the time, Pallas kernels for 0%

commit v1 on v0

--- a/solution.py
+++ b/solution.py
@@ -94,7 +94,9 @@
     local_terms = jnp.einsum(
         "bit,bct->ict", incidence, solved_cols, precision=lax.Precision.HIGHEST
     )
-    terms = lax.psum(local_terms, "front")
+    terms = local_terms
+    for hop in (1, 2):
+        terms = terms + lax.ppermute(terms, "front", [(dev, dev ^ hop) for dev in range(4)])
     weights = capacitance_solve(terms, switch_susc)
     angles = solved_cols[:, 0, :] - jnp.einsum(
         "bit,it->bt", solved_cols[:, 1:, :], weights, precision=lax.Precision.HIGHEST

time: 244 us -> 239 us (0.980)
  blocking collectives: 19.6 us -> 0 us
  waiting for transfers between devices: 118 us -> 129 us
  starting transfers between devices: 24.9 us -> 27.5 us
    psum x1 -> x0, blocking collectives: 19.6 us -> none  [body(): terms = lax.psum(local_terms, 'front')]
    ppermute x0 -> x2, waiting for transfers between devices: none -> 9.98 us  [body(): lax.ppermute(terms, 'front', [(dev, dev ^ hop) for dev in range(4)])]
    ppermute x0 -> x2, starting transfers between devices: none -> 2.53 us  [body(): lax.ppermute(terms, 'front', [(dev, dev ^ hop) for dev in range(4)])]
  transfers between devices with their start and end apart: 8 -> 10, of which waited for: 8 -> 10; matrix products, arithmetic and copies ran while one was open for 1% -> 1% of each run, Pallas kernels for 0% -> 0%
where the time goes in v1:
time: 239 us; the launch traced here: 238 us
  waiting for transfers between devices  129 us (54%)
  matrix products  34.9 us (15%)
  other arithmetic  32.6 us (14%)
  starting transfers between devices  27.5 us (12%)
  local copies, waits for them, and re-layouts  11.6 us (5%)
    ppermute x7, waiting for transfers between devices, from_behind(): return lax.ppermute(value, axis, pairs)  104 us
    dot_general x8, matrix products, product(): jnp.dot(operand, against, precision=lax.Precision.HIGHEST, preferred_elem...  29.7 us
    reduce_sum x32, other arithmetic, accumulate(): jnp.sum(centered_tanh(slot_block, in_weight, in_bias), axis=0)  23 us
    ppermute x7, starting transfers between devices, from_behind(): return lax.ppermute(value, axis, pairs)  21.5 us
    all_to_all x1, waiting for transfers between devices, body(): lax.all_to_all(outgoing, ('front', 'line'), split_axis=0, concat_axis=0,...  15.2 us
    ppermute x2, waiting for transfers between devices, body(): lax.ppermute(terms, 'front', [(dev, dev ^ hop) for dev in range(4)])  9.98 us
    sub x3, other arithmetic, upper_step(): return pivoted - arrived  6.31 us
  transfers between devices with their start and end apart: 10, of which 10 were waited for; matrix products, arithmetic and copies ran while one was open for 1% of the time, Pallas kernels for 0%

profile of v1, /device:TPU:0, one launch (start us, length us, event | category | flops | bytes accessed | tf_op | source)
XLA Modules:
  0.0 238.1 jit_solution(14995552855686193580)
XLA Ops:
  4.5 73.9 %while.32 = (s32[]{:T(128)}, f32[512,384]{1,0:T(8,128)}, f32[512,512]{1,0:T(8,128)S(1)}, f32[512,384]{1,0:T(8,128)S(1)}, s32[]{:T(128)}) while((s32[]{:T(128)}, f32[512,384]{1,0:T(8,128)}, f32[512,512]{1,0:T(8,128)S(1)}, f32[512,384]{1,0:T(8,128)S(1)}, s32[]{:T(128)}) %tuple.77), condition=%wide.region_4.0_spmd, body=%wide.region_3.0_spmd.sunk | while | flops 1208156160 | bytes 6553701 | solution.py:85
  4.5 5.8 %collective-permute-start = (f32[512,384]{1,0:T(8,128)}, f32[512,384]{1,0:T(8,128)}, u32[]{:S(2)}, u32[]{:S(2)}) collective-permute-start(f32[512,384]{1,0:T(8,128)} %get-tuple-element.274), channel_id=1, source_target_pairs={{0,4},{4,8},{8,12},{1,5},{5,9},{9,13},{2,6},{6,10},{10,14},{3,7},{... | collective-permute-start | bytes 2359304 | tf_op jit(solution)/shard_map/while/body/eval_jaxpr/ppermute | solution.py:13
  10.3 16.2 %collective-permute-done = f32[512,384]{1,0:T(8,128)} collective-permute-done((f32[512,384]{1,0:T(8,128)}, f32[512,384]{1,0:T(8,128)}, u32[]{:S(2)}, u32[]{:S(2)}) %collective-permute-start) | collective-permute-done | bytes 786464 | tf_op jit(solution)/shard_map/while/body/eval_jaxpr/ppermute | solution.py:13
  26.6 3.8 %convolution_subtract_fusion.2 = f32[512,384]{1,0:T(8,128)} fusion(f32[512,384]{1,0:T(8,128)S(1)} %get-tuple-element.281, f32[512,512]{1,0:T(8,128)S(1)} %get-tuple-element.280, f32[512,384]{1,0:T(8,128)} %collective-permute-done), kind=kOutput, calls=%fused_computation.2.clone.1 | convolution fusion | flops 1208156160 | bytes 3407872 | tf_op jit(solution)/shard_map/while/body/eval_jaxpr/dot_general | solution.py:17
  30.4 5.3 %collective-permute-start = (f32[512,384]{1,0:T(8,128)}, f32[512,384]{1,0:T(8,128)}, u32[]{:S(2)}, u32[]{:S(2)}) collective-permute-start(f32[512,384]{1,0:T(8,128)} %get-tuple-element.274), channel_id=1, source_target_pairs={{0,4},{4,8},{8,12},{1,5},{5,9},{9,13},{2,6},{6,10},{10,14},{3,7},{... | collective-permute-start | bytes 2359304 | tf_op jit(solution)/shard_map/while/body/eval_jaxpr/ppermute | solution.py:13
  35.7 15.4 %collective-permute-done = f32[512,384]{1,0:T(8,128)} collective-permute-done((f32[512,384]{1,0:T(8,128)}, f32[512,384]{1,0:T(8,128)}, u32[]{:S(2)}, u32[]{:S(2)}) %collective-permute-start) | collective-permute-done | bytes 786464 | tf_op jit(solution)/shard_map/while/body/eval_jaxpr/ppermute | solution.py:13
  51.0 3.8 %convolution_subtract_fusion.2 = f32[512,384]{1,0:T(8,128)} fusion(f32[512,384]{1,0:T(8,128)S(1)} %get-tuple-element.281, f32[512,512]{1,0:T(8,128)S(1)} %get-tuple-element.280, f32[512,384]{1,0:T(8,128)} %collective-permute-done), kind=kOutput, calls=%fused_computation.2.clone.1 | convolution fusion | flops 1208156160 | bytes 3407872 | tf_op jit(solution)/shard_map/while/body/eval_jaxpr/dot_general | solution.py:17
  54.9 5.3 %collective-permute-start = (f32[512,384]{1,0:T(8,128)}, f32[512,384]{1,0:T(8,128)}, u32[]{:S(2)}, u32[]{:S(2)}) collective-permute-start(f32[512,384]{1,0:T(8,128)} %get-tuple-element.274), channel_id=1, source_target_pairs={{0,4},{4,8},{8,12},{1,5},{5,9},{9,13},{2,6},{6,10},{10,14},{3,7},{... | collective-permute-start | bytes 2359304 | tf_op jit(solution)/shard_map/while/body/eval_jaxpr/ppermute | solution.py:13
  60.1 14.4 %collective-permute-done = f32[512,384]{1,0:T(8,128)} collective-permute-done((f32[512,384]{1,0:T(8,128)}, f32[512,384]{1,0:T(8,128)}, u32[]{:S(2)}, u32[]{:S(2)}) %collective-permute-start) | collective-permute-done | bytes 786464 | tf_op jit(solution)/shard_map/while/body/eval_jaxpr/ppermute | solution.py:13
  74.5 3.8 %convolution_subtract_fusion.2 = f32[512,384]{1,0:T(8,128)} fusion(f32[512,384]{1,0:T(8,128)S(1)} %get-tuple-element.281, f32[512,512]{1,0:T(8,128)S(1)} %get-tuple-element.280, f32[512,384]{1,0:T(8,128)} %collective-permute-done), kind=kOutput, calls=%fused_computation.2.clone.1 | convolution fusion | flops 1208156160 | bytes 3407872 | tf_op jit(solution)/shard_map/while/body/eval_jaxpr/dot_general | solution.py:17
  78.4 4.7 %convolution_bitcast_fusion = f32[512,384]{0,1:T(8,128)} fusion(f32[512,384]{1,0:T(8,128)} %get-tuple-element.98, f32[512,512]{1,0:T(8,128)S(1)} %copy-done), kind=kOutput, calls=%fused_computation.8 | convolution fusion | flops 1207959552 | bytes 2621440 | tf_op jit(solution)/shard_map/dot_general | solution.py:17
  85.4 72.7 %while.33 = (s32[]{:T(128)}, f32[512,384]{1,0:T(8,128)}, f32[512,512]{1,0:T(8,128)S(1)}, f32[512,384]{1,0:T(8,128)S(1)}, s32[]{:T(128)}) while((s32[]{:T(128)}, f32[512,384]{1,0:T(8,128)}, f32[512,512]{1,0:T(8,128)S(1)}, f32[512,384]{1,0:T(8,128)S(1)}, s32[]{:T(128)}) %tuple.78), condition=%wide.region_6.7_spmd, body=%wide.region_5.6_spmd.sunk | while | flops 1208156160 | bytes 8126565 | solution.py:92
  85.4 3.8 %fusion.37 = f32[512,384]{1,0:T(8,128)} fusion(f32[512,512]{1,0:T(8,128)S(1)} %get-tuple-element.295, f32[512,384]{1,0:T(8,128)} %get-tuple-element.289), kind=kOutput, calls=%fused_computation.57.clone.1 | convolution fusion | flops 1207959552 | bytes 2621440 | tf_op jit(solution)/shard_map/while/body/eval_jaxpr/dot_general | solution.py:17
  90.5 18.2 %collective-permute-done.1 = f32[512,384]{1,0:T(8,128)} collective-permute-done((f32[512,384]{1,0:T(8,128)}, f32[512,384]{1,0:T(8,128)}, u32[]{:S(2)}, u32[]{:S(2)}) %collective-permute-start.1) | collective-permute-done | bytes 786464 | tf_op jit(solution)/shard_map/while/body/eval_jaxpr/ppermute | solution.py:13
  110.8 3.8 %fusion.37 = f32[512,384]{1,0:T(8,128)} fusion(f32[512,512]{1,0:T(8,128)S(1)} %get-tuple-element.295, f32[512,384]{1,0:T(8,128)} %get-tuple-element.289), kind=kOutput, calls=%fused_computation.57.clone.1 | convolution fusion | flops 1207959552 | bytes 2621440 | tf_op jit(solution)/shard_map/while/body/eval_jaxpr/dot_general | solution.py:17
  116.0 16.8 %collective-permute-done.1 = f32[512,384]{1,0:T(8,128)} collective-permute-done((f32[512,384]{1,0:T(8,128)}, f32[512,384]{1,0:T(8,128)}, u32[]{:S(2)}, u32[]{:S(2)}) %collective-permute-start.1) | collective-permute-done | bytes 786464 | tf_op jit(solution)/shard_map/while/body/eval_jaxpr/ppermute | solution.py:13
  134.9 3.8 %fusion.37 = f32[512,384]{1,0:T(8,128)} fusion(f32[512,512]{1,0:T(8,128)S(1)} %get-tuple-element.295, f32[512,384]{1,0:T(8,128)} %get-tuple-element.289), kind=kOutput, calls=%fused_computation.57.clone.1 | convolution fusion | flops 1207959552 | bytes 2621440 | tf_op jit(solution)/shard_map/while/body/eval_jaxpr/dot_general | solution.py:17
  140.0 15.9 %collective-permute-done.1 = f32[512,384]{1,0:T(8,128)} collective-permute-done((f32[512,384]{1,0:T(8,128)}, f32[512,384]{1,0:T(8,128)}, u32[]{:S(2)}, u32[]{:S(2)}) %collective-permute-start.1) | collective-permute-done | bytes 786464 | tf_op jit(solution)/shard_map/while/body/eval_jaxpr/ppermute | solution.py:13
  159.5 4.5 %convolution_bitcast_fusion.1 = f32[2,3,128]{1,0,2:T(2,128)S(1)} fusion(f32[512,3,128]{0,2,1:T(8,128)S(1)} %bitcast.81, f32[512,2,128]{0,2,1:T(8,128)S(1)} %convert_subtract_fusion), kind=kOutput, calls=%fused_computation.9 | convolution fusion | flops 4718592 | bytes 1313792 | tf_op jit(solution)/shard_map/bit,bct->ict/dot_general | solution.py:94
  171.5 6.9 %collective-permute-done.3 = f32[2,3,128]{1,0,2:T(2,128)S(1)} collective-permute-done((f32[2,3,128]{1,0,2:T(2,128)S(1)}, f32[2,3,128]{1,0,2:T(2,128)S(1)}, u32[]{:S(2)}, u32[]{:S(2)}) %collective-permute-start.3) | collective-permute-done | bytes 3104 | tf_op jit(solution)/shard_map/ppermute | solution.py:99
  182.3 6.9 %collective-permute-done.4 = f32[512,128]{1,0:T(8,128)S(1)} collective-permute-done((f32[512,128]{1,0:T(8,128)S(1)}, f32[512,128]{1,0:T(8,128)S(1)}, u32[]{:S(2)}, u32[]{:S(2)}) %collective-permute-start.4) | collective-permute-done | bytes 262176 | tf_op jit(solution)/shard_map/ppermute | solution.py:13
  193.4 3.5 %all-to-all-start = ((f32[8,128,128]{2,1,0:T(8,128)}), f32[8,128,128]{2,1,0:T(8,128)S(1)}, u32[]{:S(2)}, u32[]{:S(2)}) async-start(f32[8,128,128]{2,1,0:T(8,128)} %bitcast.13), calls=%async_computation | async-start | bytes 1048576 | tf_op jit(solution)/shard_map/all_to_all | solution.py:118
  196.9 15.2 %all-to-all-done = f32[8,128,128]{2,1,0:T(8,128)S(1)} async-done(((f32[8,128,128]{2,1,0:T(8,128)}), f32[8,128,128]{2,1,0:T(8,128)S(1)}, u32[]{:S(2)}, u32[]{:S(2)}) %all-to-all-start) | async-done | bytes 524320 | tf_op jit(solution)/shard_map/all_to_all | solution.py:118
  212.2 25.2 %while.34 = (s32[]{:T(128)}, f32[128,128]{1,0:T(8,128)S(1)}, f32[32,32,128]{2,1,0:T(8,128)S(1)}, f32[128]{0:T(128)S(1)}, f32[128]{0:T(128)S(1)}, /*index=5*/f32[1,1,128]{2,1,0:T(1,128)S(1)}, s32[]{:T(128)}, s32[]{:T(128)}) while((s32[]{:T(128)}, f32[128,128]{1,0:T(8,128)S(1)}, f32[32,32,128]{2,1,0:T(8,128)S(1)}, ...), condition=%wide.region_9.10_spmd.clone, body=%wide.region_7.9_spmd.clone.sunk | while | flops 2113539 | bytes 312931 | solution.py:127
  (165 shorter events, 57.6 us)
Async XLA Ops:
  0.6 77.8 %copy-start = (f32[512,512]{1,0:T(8,128)S(1)}, f32[512,512]{1,0:T(8,128)}, u32[]{:S(2)}) copy-start(f32[512,512]{1,0:T(8,128)} %param.24) | copy-start | bytes 3145732
  3.0 1.5 copy-start.1
  4.5 22.0 %collective-permute-start = (f32[512,384]{1,0:T(8,128)}, f32[512,384]{1,0:T(8,128)}, u32[]{:S(2)}, u32[]{:S(2)}) collective-permute-start(f32[512,384]{1,0:T(8,128)} %get-tuple-element.274), channel_id=1, source_target_pairs={{0,4},{4,8},{8,12},{1,5},{5,9},{9,13},{2,6},{6,10},{10,14},{3,7},{... | collective-permute-start | bytes 2359304 | tf_op jit(solution)/shard_map/while/body/eval_jaxpr/ppermute | solution.py:13
  30.4 20.6 %collective-permute-start = (f32[512,384]{1,0:T(8,128)}, f32[512,384]{1,0:T(8,128)}, u32[]{:S(2)}, u32[]{:S(2)}) collective-permute-start(f32[512,384]{1,0:T(8,128)} %get-tuple-element.274), channel_id=1, source_target_pairs={{0,4},{4,8},{8,12},{1,5},{5,9},{9,13},{2,6},{6,10},{10,14},{3,7},{... | collective-permute-start | bytes 2359304 | tf_op jit(solution)/shard_map/while/body/eval_jaxpr/ppermute | solution.py:13
  54.9 19.7 %collective-permute-start = (f32[512,384]{1,0:T(8,128)}, f32[512,384]{1,0:T(8,128)}, u32[]{:S(2)}, u32[]{:S(2)}) collective-permute-start(f32[512,384]{1,0:T(8,128)} %get-tuple-element.274), channel_id=1, source_target_pairs={{0,4},{4,8},{8,12},{1,5},{5,9},{9,13},{2,6},{6,10},{10,14},{3,7},{... | collective-permute-start | bytes 2359304 | tf_op jit(solution)/shard_map/while/body/eval_jaxpr/ppermute | solution.py:13
  89.2 19.5 %collective-permute-start.1 = (f32[512,384]{1,0:T(8,128)}, f32[512,384]{1,0:T(8,128)}, u32[]{:S(2)}, u32[]{:S(2)}) collective-permute-start(f32[512,384]{1,0:T(8,128)} %fusion.37), channel_id=1, source_target_pairs={{4,0},{8,4},{12,8},{5,1},{9,5},{13,9},{6,2},{10,6},{14,10},{7,3},{... | collective-permute-start | bytes 2359304 | tf_op jit(solution)/shard_map/while/body/eval_jaxpr/ppermute | solution.py:13
  114.7 18.1 %collective-permute-start.1 = (f32[512,384]{1,0:T(8,128)}, f32[512,384]{1,0:T(8,128)}, u32[]{:S(2)}, u32[]{:S(2)}) collective-permute-start(f32[512,384]{1,0:T(8,128)} %fusion.37), channel_id=1, source_target_pairs={{4,0},{8,4},{12,8},{5,1},{9,5},{13,9},{6,2},{10,6},{14,10},{7,3},{... | collective-permute-start | bytes 2359304 | tf_op jit(solution)/shard_map/while/body/eval_jaxpr/ppermute | solution.py:13
  138.7 17.2 %collective-permute-start.1 = (f32[512,384]{1,0:T(8,128)}, f32[512,384]{1,0:T(8,128)}, u32[]{:S(2)}, u32[]{:S(2)}) collective-permute-start(f32[512,384]{1,0:T(8,128)} %fusion.37), channel_id=1, source_target_pairs={{4,0},{8,4},{12,8},{5,1},{9,5},{13,9},{6,2},{10,6},{14,10},{7,3},{... | collective-permute-start | bytes 2359304 | tf_op jit(solution)/shard_map/while/body/eval_jaxpr/ppermute | solution.py:13
  159.4 5.8 %copy-start.4 = (s32[512,1]{0,1:T(1,128)S(1)}, s32[512,1]{0,1:T(1,128)}, u32[]{:S(2)}) copy-start(s32[512,1]{0,1:T(1,128)} %param.28) | copy-start | bytes 6148
  159.4 7.3 %copy-start.6 = (s32[512]{0:T(512)S(1)}, s32[512]{0:T(512)}, u32[]{:S(2)}) copy-start(s32[512]{0:T(512)} %param.26) | copy-start | bytes 6148
  159.5 7.3 %copy-start.7 = (s32[512]{0:T(512)S(1)}, s32[512]{0:T(512)}, u32[]{:S(2)}) copy-start(s32[512]{0:T(512)} %param.25) | copy-start | bytes 6148
  164.0 6.0 %collective-permute-start.2 = (f32[2,3,128]{1,0,2:T(2,128)S(1)}, f32[2,3,128]{1,0,2:T(2,128)S(1)}, u32[]{:S(2)}, u32[]{:S(2)}) collective-permute-start(f32[2,3,128]{1,0,2:T(2,128)S(1)} %convolution_bitcast_fusion.1), channel_id=1, source_target_pairs={{0,4},{4,0},{8,12},{12,8},{1,5},{5,1},{9,13},{13,9},{2,6},{6,2},{1... | collective-permute-start | bytes 9224 | tf_op jit(solution)/shard_map/ppermute | solution.py:99
  166.9 13.8 %copy-start.8 = (f32[2,128]{1,0:T(2,128)S(1)}, f32[2,128]{1,0:T(2,128)}, u32[]{:S(2)}) copy-start(f32[2,128]{1,0:T(2,128)} %param.22) | copy-start | bytes 3076
  170.0 8.4 %collective-permute-start.3 = (f32[2,3,128]{1,0,2:T(2,128)S(1)}, f32[2,3,128]{1,0,2:T(2,128)S(1)}, u32[]{:S(2)}, u32[]{:S(2)}) collective-permute-start(f32[2,3,128]{1,0,2:T(2,128)S(1)} %add.66), channel_id=1, source_target_pairs={{0,8},{4,12},{8,0},{12,4},{1,9},{5,13},{9,1},{13,5},{2,10},{6,14},... | collective-permute-start | bytes 9224 | tf_op jit(solution)/shard_map/ppermute | solution.py:99
  181.0 9.4 %copy-start.2 = (f32[512,128]{1,0:T(8,128)}, f32[512,128]{1,0:T(8,128)S(1)}, u32[]{:S(2)}) copy-start(f32[512,128]{1,0:T(8,128)S(1)} %bitcast_subtract_fusion) | copy-start | bytes 786436
  181.0 8.3 %collective-permute-start.4 = (f32[512,128]{1,0:T(8,128)S(1)}, f32[512,128]{1,0:T(8,128)S(1)}, u32[]{:S(2)}, u32[]{:S(2)}) collective-permute-start(f32[512,128]{1,0:T(8,128)S(1)} %bitcast_subtract_fusion), channel_id=1, source_target_pairs={{4,0},{8,4},{12,8},{5,1},{9,5},{13,9},{6,2},{10,6},{14,10},{7,3},{... | collective-permute-start | bytes 786440 | tf_op jit(solution)/shard_map/ppermute | solution.py:13
  190.4 1.1 copy-start.5
  191.4 5.5 %copy-start.10 = (f32[128]{0:T(128)S(1)}, f32[128]{0:T(128)}, u32[]{:S(2)}) copy-start(f32[128]{0:T(128)} %param.30) | copy-start | bytes 1540
  191.4 20.7 %copy-start.9 = (f32[128]{0:T(128)S(1)}, f32[128]{0:T(128)}, u32[]{:S(2)}) copy-start(f32[128]{0:T(128)} %param.29) | copy-start | bytes 1540
  193.4 18.8 %all-to-all-start = ((f32[8,128,128]{2,1,0:T(8,128)}), f32[8,128,128]{2,1,0:T(8,128)S(1)}, u32[]{:S(2)}, u32[]{:S(2)}) async-start(f32[8,128,128]{2,1,0:T(8,128)} %bitcast.13), calls=%async_computation | async-start | bytes 1048576 | tf_op jit(solution)/shard_map/all_to_all | solution.py:118
  212.2 25.2 %copy-start.3 = (bf16[128,128]{1,0:T(8,128)(2,1)S(1)}, bf16[128,128]{1,0:T(8,128)(2,1)}, u32[]{:S(2)}) copy-start(bf16[128,128]{1,0:T(8,128)(2,1)} %param.31) | copy-start | bytes 98308
